TPU v7x, 32 devices: a whole 2x2x4 slice. The times are simulated.
32 devices in a mesh: dp: 8 (over z, y), rep: 2 (over x), cores: 2 (over core).
Axes of the slice: x: 2, y: 2, z: 4, core: 2. Of those that a mesh axis runs over, the one named last changes fastest.
Arguments:
- tokens: bfloat16 [16384, 1024], P(('dp', 'rep', 'cores')), may hold values from -6 to 6
- norm_attn: bfloat16 [1024], P('dp'), may hold values from 0.5 to 1.5
- w_query: bfloat16 [1024, 1024], P('dp'), may hold values from -0.1875 to 0.1875
- w_key: bfloat16 [1024, 1024], P('dp'), may hold values from -0.1875 to 0.1875
- w_value: bfloat16 [1024, 1024], P('dp'), may hold values from -0.1875 to 0.1875
- w_out: bfloat16 [1024, 1024], P('dp'), may hold values from -0.75 to 0.75
- norm_ffn: bfloat16 [1024], P('dp'), may hold values from 0.5 to 1.5
- w_gate: bfloat16 [1024, 2816], P('dp'), may hold values from -0.1875 to 0.1875
- w_up: bfloat16 [1024, 2816], P('dp'), may hold values from -0.1875 to 0.1875
- w_down: bfloat16 [2816, 1024], P('dp'), may hold values from -0.109375 to 0.109375
- lengths: int32 [32, 1], P(('dp', 'rep', 'cores')), may hold values from 384 to 512, as said below
- cotangent: bfloat16 [16384, 1024], P(('dp', 'rep', 'cores')), may hold values from -6 to 6
Outputs:
- mixed: bfloat16 [16384, 1024], P(('dp', 'rep', 'cores'))
- input_grad: float32 [16384, 1024], P(('dp', 'rep', 'cores'))
- grad_norm_attn: float32 [1024], P('dp')
- grad_query: float32 [1024, 1024], P('dp')
- grad_key: float32 [1024, 1024], P('dp')
- grad_value: float32 [1024, 1024], P('dp')
- grad_out: float32 [1024, 1024], P('dp')
- grad_norm_ffn: float32 [1024], P('dp')
- grad_gate: float32 [1024, 2816], P('dp')
- grad_up: float32 [1024, 2816], P('dp')
- grad_down: float32 [2816, 1024], P('dp')
Inputs may be any that keep to these rules, and one draw needn't show every extreme that they name: Block b holds one whole sequence of lengths[b] patches from its first slot; the remaining slots are padding. The sequence in block 0 fills all 512 slots.
All inputs are finite; a program needn't handle non-finite values.
Results may differ from a plain program's by a relative error of at most 0.017.
Values may be sent and summed in bfloat16 or wider, within the bound.
A program may use at most 192 MiB of HBM per device.

v0:
```python
from functools import partial

import jax
import jax.numpy as jnp
from jax import lax
from jax.experimental import pallas as pl
from jax.experimental.pallas import tpu as pltpu
from jax.sharding import PartitionSpec as P

HEADS = 16
HEAD = 64


NORM_EPS = 1e-05
SCORE_SCALE = 0.125
NEGATIVE = -1e30
head_group = 4
MESH = pl.DeviceIdType.MESH
MIB = 1024 * 1024


def masks(block_len, rows):
    bounds = jnp.cumsum(block_len[0])
    place = jnp.arange(rows, dtype=jnp.int32)
    segment = jnp.sum((place[:, None] >= bounds[None, :]).astype(jnp.int32), axis=1)
    allowed = (segment[:, None] == segment[None, :]) & (place[None, :] <= place[:, None])
    valid = (segment < block_len.shape[1]).astype(jnp.float32)
    return (allowed, valid)


def normalize(values):
    factor = lax.rsqrt(jnp.mean(values * values, axis=-1, keepdims=True) + NORM_EPS)
    return (values * factor, factor)


def norm_back(grad_normed, normed, factor):
    return factor * (grad_normed - normed * jnp.mean(grad_normed * normed, axis=-1, keepdims=True))


def matmul(left, right):
    return jnp.dot(left, right, preferred_element_type=jnp.float32)


def matmul_tn(left, right):
    return lax.dot_general(
        left, right, (((0,), (0,)), ((), ())), preferred_element_type=jnp.float32
    )


def matmul_nt(left, right):
    return lax.dot_general(
        left, right, (((1,), (1,)), ((), ())), preferred_element_type=jnp.float32
    )


def to_groups(matrix):
    rows = matrix.shape[0]
    split = matrix.reshape(rows, HEADS // head_group, head_group, HEAD)
    return split.transpose(1, 2, 0, 3)


def from_groups(grouped):
    rows = grouped.shape[2]
    return grouped.transpose(2, 0, 1, 3).reshape(rows, HEADS * HEAD)


def group_scores(allowed, query_g, key_g):
    raw = (
        jnp.einsum("hqe,hke->hqk", query_g, key_g, preferred_element_type=jnp.float32) * SCORE_SCALE
    )
    return jnp.where(allowed[None], raw, NEGATIVE)


def attend(allowed, operands):
    query_g, key_g, value_g = operands
    scores = group_scores(allowed, query_g, key_g)
    top = jnp.max(scores, axis=-1, keepdims=True)
    expo = jnp.exp(scores - top)
    total = jnp.sum(expo, axis=-1, keepdims=True)
    probs_low = (expo / total).astype(jnp.bfloat16)
    result = jnp.einsum("hqk,hke->hqe", probs_low, value_g, preferred_element_type=jnp.float32)
    return (result.astype(jnp.bfloat16), top[..., 0] + jnp.log(total[..., 0]))


def attend_back(allowed, operands):
    query_g, key_g, value_g, grad_g, lse = operands
    scores = group_scores(allowed, query_g, key_g)
    probs = jnp.exp(scores - lse[..., None])
    grad_probs = jnp.einsum("hqe,hke->hqk", grad_g, value_g, preferred_element_type=jnp.float32)
    centre = jnp.sum(grad_probs * probs, axis=-1, keepdims=True)
    grad_scores = (probs * (grad_probs - centre)).astype(jnp.bfloat16)
    grad_query = (
        jnp.einsum("hqk,hke->hqe", grad_scores, key_g, preferred_element_type=jnp.float32)
        * SCORE_SCALE
    )
    grad_key = (
        jnp.einsum("hqk,hqe->hke", grad_scores, query_g, preferred_element_type=jnp.float32)
        * SCORE_SCALE
    )
    grad_value = jnp.einsum(
        "hqk,hqe->hke", probs.astype(jnp.bfloat16), grad_g, preferred_element_type=jnp.float32
    )
    return (
        grad_query.astype(jnp.bfloat16),
        grad_key.astype(jnp.bfloat16),
        grad_value.astype(jnp.bfloat16),
    )


class Part:
    def __init__(self, weight, tall, start, size, no_x):
        self.weight, self.tall, self.start, self.size = weight, tall, start, size
        self.no_x = no_x

    def quarter(self, ref, lead, c, x):
        if self.tall:
            columns = pl.ds(pl.multiple_of(c * 512 + x * 256, 256), 256)
            return ref.at[(*lead, pl.ds(self.start, self.size), columns)]
        return ref.at[(*lead, x, slice(None), self.columns(c))]

    def half(self, ref, lead, c):
        if self.tall:
            columns = pl.ds(pl.multiple_of(c * 512, 512), 512)
            return ref.at[(*lead, pl.ds(self.start, self.size), columns)]
        return ref.at[(*lead, slice(None), slice(None), self.columns(c))]

    def columns(self, c):
        width = self.size // 2
        return pl.ds(pl.multiple_of(self.start + c * width, 128), width)


def pieces(total, most):
    return [(start, min(most, total - start)) for start in range(0, total, most)]


def place():
    d = lax.axis_index("dp")
    return lax.div(d, 2), lax.rem(d, 2), lax.axis_index("rep"), lax.axis_index("cores")


def device(z, y, x, c):
    return {"dp": 2 * z + y, "rep": x, "cores": c}


def greet():
    z, y, x, c = place()
    barrier = pltpu.get_barrier_semaphore()
    others = [device(lax.rem(z + k, 4), y, x, c) for k in (1, 2, 3)]
    others += [device(z, 1 - y, x, c), device(z, y, 1 - x, c), device(z, y, x, 1 - c)]
    for other in others:
        pl.semaphore_signal(barrier, inc=1, device_id=other, device_id_type=MESH)
    pl.semaphore_wait(barrier, len(others))


class Wires:
    def __init__(self, send_sems, recv_sems):
        self.send_sems, self.recv_sems, self.sent = send_sems, recv_sems, []

    def copy(self, slot, source, target, other):
        return pltpu.make_async_remote_copy(
            src_ref=source,
            dst_ref=target,
            send_sem=self.send_sems.at[slot],
            recv_sem=self.recv_sems.at[slot],
            device_id=other,
            device_id_type=MESH,
        )

    def send(self, slot, source, target, other):
        copy = self.copy(slot, source, target, other)
        copy.start()
        self.sent.append((slot, copy))

    def arrived(self, slot, target):
        z, y, x, c = place()
        self.copy(slot, target, target, device(z, y, x, 1 - c)).wait_recv()

    def finish(self, chosen=lambda slot: True):
        for slot, copy in self.sent:
            if chosen(slot):
                copy.wait_send()
        self.sent = [(slot, copy) for slot, copy in self.sent if not chosen(slot)]


GATHER_SLOTS = 12
LAG = 2
ALL = slice(None)
COLUMNS = (1024, 1024, 1024, 1024, 2816, 2816, None)
QUERY, KEY, VALUE, OUT, GATE, UP, DOWN = range(7)
TILE = 512


FF_CHUNKS = tuple(pieces(2816, 512))


def gather_items():
    order = [(QUERY, 0, 256, True), (QUERY, 256, 768, False), (KEY, 0, 1024, True)]
    order += [(VALUE, 0, 1024, False), (OUT, 0, 1024, False)]
    order += [(DOWN, 0, 128, False), (DOWN, 128, 128, True), (DOWN, 256, 96, False)]
    for n, (start, size) in enumerate(FF_CHUNKS):
        order += [(GATE, start, size, n == 5), (UP, start, size, n in (0, 3, 5))]
    return [Part(w, w == DOWN, start, size, no_x) for w, start, size, no_x in order]


def dot(left, right):
    return lax.dot_general(
        left, right, (((1,), (0,)), ((), ())), preferred_element_type=jnp.float32
    )


def dot_nt(left, right):
    return lax.dot_general(
        left, right, (((1,), (1,)), ((), ())), preferred_element_type=jnp.float32
    )


def tile(index, size):
    return pl.ds(pl.multiple_of(index * size, size), size)


def weight_columns(ref, at):
    return ref[:, :, :, :, at].reshape(1024, -1)


class Forward:
    def __init__(self, refs):
        self.__dict__.update(refs)

    def prepare(self):
        for s in range(8):
            self.gain[:, 128 * s : 128 * s + 128] = self.gains[s // 2, s % 2]
        length = self.length[0, 0]
        for block in range(4):
            rows = slice(128 * block, 128 * block + 128)
            place_q = lax.broadcasted_iota(jnp.int32, (128, 512), 0) + 128 * block
            place_k = lax.broadcasted_iota(jnp.int32, (128, 512), 1)
            same = (place_q >= length) == (place_k >= length)
            allowed = same & (place_k <= place_q)
            self.bias[rows, :] = jnp.where(allowed, 0.0, NEGATIVE)

        def normed(block, _):
            rows = tile(block, 64)
            values = self.tokens[rows, :].astype(jnp.float32)
            factor = lax.rsqrt(jnp.mean(values * values, axis=-1, keepdims=True) + NORM_EPS)
            gain = self.gain[0:1, :].astype(jnp.float32)
            self.hidden[rows, :] = (values * factor * gain).astype(jnp.bfloat16)
            place = lax.broadcasted_iota(jnp.int32, (64, 1024), 0) + 64 * block
            d_b = jnp.where(place < length, self.cotangent[rows, :].astype(jnp.float32), 0.0)
            self.d_b[rows, :] = d_b.astype(jnp.bfloat16)
            return 0

        lax.fori_loop(0, 8, normed, 0)
        self.turn(self.hidden, self.h_t)
        self.out("d_b")

    def turn(self, matrix, turned):
        def columns(n, _):
            at = tile(n, 128)
            turned[at, :] = matrix[:, at].astype(jnp.float32).T.astype(jnp.bfloat16)
            return 0

        lax.fori_loop(0, 8, columns, 0)

    def project(self, weight, result):
        def columns(n, _):
            at = tile(n, TILE)
            result[:, at] = dot(self.hidden[...], weight_columns(weight, at)).astype(jnp.bfloat16)
            return 0

        lax.fori_loop(0, 1024 // TILE, columns, 0)

    def attend(self, first, last):
        def pair(p, _):
            at = tile(p, 128)
            left = lax.broadcasted_iota(jnp.int32, (256, 128), 1) < HEAD
            for block in (0, 1):
                rows, seen = slice(256 * block, 256 * block + 256), slice(0, 256 * block + 256)
                query = self.query[rows, at].astype(jnp.float32) * SCORE_SCALE
                both = jnp.concatenate(
                    [jnp.where(left, query, 0.0), jnp.where(left, 0.0, query)], axis=0
                ).astype(jnp.bfloat16)
                bias = self.bias[rows, seen]
                scores = dot_nt(both, self.key[seen, at]) + jnp.concatenate([bias, bias], axis=0)
                top = jnp.max(scores, axis=-1, keepdims=True)
                expo = jnp.exp(scores - top)
                total = jnp.sum(expo, axis=-1, keepdims=True)
                probs = (expo * (1.0 / total)).astype(jnp.bfloat16)
                result = dot(probs, self.value[seen, at])
                self.attended[rows, at] = jnp.where(left, result[:256], result[256:]).astype(
                    jnp.bfloat16
                )
                lse = top + jnp.log(total)
                turned = jnp.where(left, lse[:256], lse[256:]).T
                self.lse[p, 0:1, rows] = turned[0:1]
                self.lse[p, 1:2, rows] = turned[HEAD : HEAD + 1]
            return 0

        lax.fori_loop(first, last, pair, 0)

    def project_out(self):
        def columns(n, _):
            at = tile(n, TILE)
            self.residual[:, at] = self.tokens[:, at].astype(jnp.float32) + dot(
                self.attended[...], weight_columns(self.w_out, at)
            )
            return 0

        lax.fori_loop(0, 1024 // TILE, columns, 0)

        def normed(block, _):
            rows = tile(block, 64)
            values = self.residual[rows, :]
            factor = lax.rsqrt(jnp.mean(values * values, axis=-1, keepdims=True) + NORM_EPS)
            gain = self.gain[8:9, :].astype(jnp.float32)
            self.h2[rows, :] = (values * factor * gain).astype(jnp.bfloat16)
            return 0

        lax.fori_loop(0, 8, normed, 0)
        self.turn(self.h2, self.h2_t)
        self.turn(self.attended, self.att_t)
        for name in ("query", "key", "value", "lse", "h_t", "h2_t", "att_t"):
            self.out(name)

    def grad_of_middle(self, start, size):
        at = pl.ds(start, size)
        self.d_up[:, at] = dot_nt(self.d_b[...], self.w_down[at, :]).astype(jnp.bfloat16)

    def feed_forward(self, start, size):
        at = pl.ds(start, size)
        low = jnp.bfloat16
        gate_w = weight_columns(self.w_gate, at)
        up_w = weight_columns(self.w_up, at)
        down_w = self.w_down[at, :]
        gate = dot(self.h2[...], gate_w)
        upward = dot(self.h2[...], up_w)
        grad_middle = self.d_up[:, at].astype(jnp.float32)
        sigma = 0.5 * jnp.tanh(0.5 * gate) + 0.5
        silu = gate * sigma
        mid = (silu * upward).astype(low)
        d_up = (grad_middle * silu).astype(low)
        d_gate = (grad_middle * upward * (sigma + silu - silu * sigma)).astype(low)
        self.mid[:, at] = mid
        self.d_up[:, at] = d_up
        self.d_gate[:, at] = d_gate
        for j in range(1024 // TILE):
            part = slice(TILE * j, TILE * j + TILE)
            mixed = dot(mid, down_w[:, part])
            grad = dot_nt(d_gate, gate_w[part, :]) + dot_nt(d_up, up_w[part, :])
            if start == 0:
                self.total[:, part] = mixed
                self.d_h2[:, part] = grad
            else:
                self.total[:, part] += mixed
                self.d_h2[:, part] += grad

    def flush(self, start, size):
        for name in ("mid", "d_gate", "d_up"):
            self.out(name, pl.ds(start, size))

    def finish(self):
        length = self.length[0, 0]
        self.g_ffn[...] = jnp.zeros_like(self.g_ffn)

        def rows_of(block, _):
            rows = tile(block, 64)
            place = lax.broadcasted_iota(jnp.int32, (64, 1024), 0) + 64 * block
            residual = self.residual[rows, :]
            mixed = jnp.where(place < length, residual + self.total[rows, :], 0.0)
            self.mixed[rows, :] = mixed.astype(jnp.bfloat16)
            factor = lax.rsqrt(jnp.mean(residual * residual, axis=-1, keepdims=True) + NORM_EPS)
            normed = residual * factor
            grad = self.d_h2[rows, :]
            self.g_ffn[...] += jnp.sum((grad * normed).reshape(8, 8, 1024), axis=0)
            grad_normed = grad * self.gain[8:9, :].astype(jnp.float32)
            grad_out = jnp.where(place < length, self.cotangent[rows, :].astype(jnp.float32), 0.0)
            mean = jnp.mean(grad_normed * normed, axis=-1, keepdims=True)
            d_res = grad_out + factor * (grad_normed - normed * mean)
            self.d_res[rows, :] = d_res
            self.d_proj[rows, :] = d_res.astype(jnp.bfloat16)
            return 0

        lax.fori_loop(0, 8, rows_of, 0)
        for name in ("mixed", "d_res", "d_proj", "g_ffn", "gain"):
            self.out(name)


FORWARD_OUTS = (
    ("mixed", (512, 1024), jnp.bfloat16),
    ("query", (512, 1024), jnp.bfloat16),
    ("key", (512, 1024), jnp.bfloat16),
    ("value", (512, 1024), jnp.bfloat16),
    ("lse", (8, 8, 512), jnp.float32),
    ("h_t", (1024, 512), jnp.bfloat16),
    ("h2_t", (1024, 512), jnp.bfloat16),
    ("att_t", (1024, 512), jnp.bfloat16),
    ("d_b", (512, 1024), jnp.bfloat16),
    ("mid", (512, 2816), jnp.bfloat16),
    ("d_gate", (512, 2816), jnp.bfloat16),
    ("d_up", (512, 2816), jnp.bfloat16),
    ("d_res", (512, 1024), jnp.float32),
    ("d_proj", (512, 1024), jnp.bfloat16),
    ("g_ffn", (8, 1024), jnp.float32),
    ("gain", (16, 1024), jnp.bfloat16),
)
FORWARD_OWN = (
    ("hidden", (512, 1024), jnp.bfloat16),
    ("attended", (512, 1024), jnp.bfloat16),
    ("residual", (512, 1024), jnp.float32),
    ("h2", (512, 1024), jnp.bfloat16),
    ("d_h2", (512, 1024), jnp.float32),
    ("bias", (512, 512), jnp.float32),
    ("total", (512, 1024), jnp.float32),
)
OUT_COPIES = len(FORWARD_OUTS) - 3 + 3 * len(FF_CHUNKS)
KEPT = (QUERY, KEY, VALUE, OUT)


def share_shape(columns):
    return (352, 1024) if columns is None else (2, 64, columns)


def forward_kernel(items, *refs):
    refs = list(refs)

    def take(n):
        taken = refs[:n]
        del refs[:n]
        return taken

    shares = take(7)
    gain_attn, gain_ffn, tokens, cotangent, length = take(5)
    kept = take(len(KEPT))
    names = [name for name, _, _ in FORWARD_OUTS]
    outs = dict(zip(names, take(len(names))))
    full = take(7)
    full_gains, gains = take(2)
    own_names = names + [name for name, _, _ in FORWARD_OWN]
    state = dict(zip(own_names, take(len(own_names))))
    send_sems, recv_sems, own_sems, keep_sems, out_sems = refs
    outgoing = []

    def put(name, columns=None):
        source, target = state[name], outs[name]
        if columns is not None:
            source, target = source.at[:, columns], target.at[:, columns]
        outgoing.append(pltpu.make_async_copy(source, target, out_sems.at[len(outgoing)]))
        outgoing[-1].start()

    z, y, x, c = place()
    far = [lax.rem(z + k, 4) for k in range(4)]
    back = [lax.rem(z + 4 - k, 4) for k in range(4)]
    x_other, y_other, c_other = (
        device(z, y, 1 - x, c),
        device(z, 1 - y, x, c),
        device(z, y, x, 1 - c),
    )
    greet()
    wires = Wires(send_sems, recv_sems)
    own = [
        pltpu.make_async_copy(share, whole.at[z, y], own_sems.at[i])
        for i, (share, whole) in enumerate(zip(shares, full))
    ]
    own_gains = pltpu.make_async_copy(gains, full_gains.at[z, y], own_sems.at[7])
    keep = [
        pltpu.make_async_copy(full[w], kept[n], keep_sems.at[n]) for n, w in enumerate(KEPT)
    ]
    gains[...] = jnp.where(
        lax.broadcasted_iota(jnp.int32, (16, 128), 0) < 8,
        jnp.broadcast_to(gain_attn[...].astype(jnp.float32), (16, 128)),
        jnp.broadcast_to(gain_ffn[...].astype(jnp.float32), (16, 128)),
    ).astype(jnp.bfloat16)
    own_gains.start()
    gain_slot = GATHER_SLOTS * len(items)
    for k in (1, 2, 3):
        wires.send(gain_slot + k, gains, full_gains.at[z, y], device(far[k], y, x, c))
    for copy in own:
        copy.start()

    def slot(i, k):
        return GATHER_SLOTS * i + k

    def along_z(i):
        item = items[i]
        share, whole = shares[item.weight], full[item.weight]
        for k in (1, 2, 3):
            if item.no_x:
                source, target = item.half(share, (), c), item.half(whole, (z, y), c)
            else:
                source, target = item.quarter(share, (), c, x), item.quarter(whole, (z, y), c, x)
            wires.send(slot(i, k), source, target, device(far[k], y, x, c))

    own_done = set()

    def first_hop(i):
        item = items[i]
        whole = full[item.weight]
        if item.weight not in own_done:
            own[item.weight].wait()
            own_done.add(item.weight)
        for k in (1, 2, 3):
            if item.no_x:
                block = item.half(whole, (back[k], y), c)
                wires.arrived(slot(i, k), block)
                wires.send(slot(i, 7 + k), block, block, c_other)
            else:
                block = item.quarter(whole, (back[k], y), c, x)
                wires.arrived(slot(i, k), block)
                wires.send(slot(i, 3 + k), block, block, x_other)
        if item.no_x:
            block = item.half(whole, (ALL, y), c)
        else:
            block = item.quarter(whole, (ALL, y), c, x)
        wires.send(slot(i, 7), block, block, y_other)

    def second_hop(i):
        item = items[i]
        whole = full[item.weight]
        if item.no_x:
            block = item.half(whole, (ALL, 1 - y), c)
            wires.arrived(slot(i, 7), block)
            wires.send(slot(i, 11), block, block, c_other)
            return
        block = item.quarter(whole, (ALL, 1 - y), c, x)
        wires.arrived(slot(i, 7), block)
        wires.send(slot(i, 0), block, block, x_other)
        for k in (1, 2, 3):
            wires.arrived(slot(i, 3 + k), item.quarter(whole, (back[k], y), c, 1 - x))
        for k in (1, 2, 3):
            block = item.half(whole, (back[k], y), c)
            wires.send(slot(i, 7 + k), block, block, c_other)

    def last_hop(i):
        item = items[i]
        whole = full[item.weight]
        if not item.no_x:
            block = item.half(whole, (ALL, 1 - y), c)
            wires.arrived(slot(i, 0), item.quarter(whole, (ALL, 1 - y), c, 1 - x))
            wires.send(slot(i, 11), block, block, c_other)

    def complete(i):
        item = items[i]
        whole = full[item.weight]
        for k in (1, 2, 3):
            wires.arrived(slot(i, 7 + k), item.half(whole, (back[k], y), 1 - c))
        wires.arrived(slot(i, 11), item.half(whole, (ALL, 1 - y), 1 - c))

    def retire(i):
        wires.finish(lambda slot: slot // GATHER_SLOTS == i)

    step_of = Forward(
        dict(
            state,
            out=put,
            tokens=tokens,
            cotangent=cotangent,
            length=length,
            gains=full_gains,
            w_out=full[OUT],
            w_gate=full[GATE],
            w_up=full[UP],
            w_down=full[DOWN].reshape(2816, 1024),
        )
    )
    last_of = {item.weight: i for i, item in enumerate(items)}
    tasks = [(-1, 3, step_of.prepare)]
    for n, name in enumerate(("query", "key", "value")):
        tasks.append((last_of[n], 2, partial(step_of.project, full[n], state[name])))
    tasks += [(last_of[VALUE], 3, partial(step_of.attend, p, p + 2)) for p in (0, 2, 4, 6)]
    tasks.append((last_of[OUT], 3, step_of.project_out))
    for tile_of in pieces(2816, TILE):
        tasks.append((last_of[DOWN], 1, partial(step_of.grad_of_middle, *tile_of)))
    for start, size in FF_CHUNKS:
        there = max(
            i for i, item in enumerate(items) if item.weight == UP and item.start == start
        )
        for at, width in pieces(size, TILE):
            tasks.append((there, 5, partial(step_of.feed_forward, start + at, width)))
        tasks.append((there, 0, partial(step_of.flush, start, size)))

    ahead = 3
    for i in range(min(ahead, len(items))):
        along_z(i)
    own_gains.wait()
    for k in (1, 2, 3):
        wires.arrived(gain_slot + k, full_gains.at[back[k], y])
    wires.send(gain_slot, full_gains.at[:, y], full_gains.at[:, y], y_other)
    stages = (retire, complete, last_hop, second_hop, first_hop)
    lates = (3 * LAG, 3 * LAG - 1, 2 * LAG, LAG, 0)
    for step in range(len(items) + 3 * LAG):
        for late, stage in zip(lates, stages):
            if 0 <= step - late < len(items):
                stage(step - late)
        if step + ahead < len(items):
            along_z(step + ahead)
        if step == 0:
            wires.arrived(gain_slot, full_gains.at[:, 1 - y])
        there = step - lates[1]
        for n, w in enumerate(KEPT):
            if there == last_of[w]:
                keep[n].start()
        spent = 0
        while tasks and tasks[0][0] <= there and spent < 6:
            _, cost, task = tasks.pop(0)
            task()
            spent += cost
    for _, _, task in tasks:
        task()
    step_of.finish()
    for copy in keep + outgoing:
        copy.wait()
    wires.finish()


def forward(tokens, cotangent, lengths, weights, gains):
    items = gather_items()
    shares = [w.reshape(share_shape(n)) for w, n in zip(weights, COLUMNS)]
    wholes = [(4, 2) + share_shape(n) for n in COLUMNS]
    shapes = [jax.ShapeDtypeStruct(wholes[w], jnp.bfloat16) for w in KEPT]
    shapes += [jax.ShapeDtypeStruct(shape, dtype) for _, shape, dtype in FORWARD_OUTS]
    count = GATHER_SLOTS * len(items) + 4
    anywhere = pl.BlockSpec(memory_space=pl.ANY)
    in_vmem = pl.BlockSpec(memory_space=pltpu.VMEM)
    out = pl.pallas_call(
        partial(forward_kernel, items),
        out_shape=shapes,
        in_specs=[anywhere] * 7
        + [in_vmem] * 4
        + [pl.BlockSpec(memory_space=pltpu.SMEM)],
        out_specs=[anywhere] * len(shapes),
        scratch_shapes=[pltpu.VMEM(shape, jnp.bfloat16) for shape in wholes]
        + [pltpu.VMEM((4, 2, 16, 128), jnp.bfloat16), pltpu.VMEM((16, 128), jnp.bfloat16)]
        + [pltpu.VMEM(shape, dtype) for _, shape, dtype in FORWARD_OUTS + FORWARD_OWN]
        + [
            pltpu.SemaphoreType.DMA((count,)),
            pltpu.SemaphoreType.DMA((count,)),
            pltpu.SemaphoreType.DMA((8,)),
            pltpu.SemaphoreType.DMA((len(KEPT),)),
            pltpu.SemaphoreType.DMA((OUT_COPIES,)),
        ],
        compiler_params=pltpu.CompilerParams(
            collective_id=0, has_side_effects=True, vmem_limit_bytes=63 * MIB
        ),
        name="gather_forward",
    )(*shares, *[g.reshape(1, 128) for g in gains], tokens, cotangent, lengths)
    return out[: len(KEPT)], dict(zip([name for name, _, _ in FORWARD_OUTS], out[len(KEPT) :]))


SUM_SLOTS = 10
RING = 4


class Share:
    def __init__(self, weight, start, size, x_first):
        self.weight, self.start, self.size, self.x_first = weight, start, size, x_first
        self.tall = weight == DOWN
        self.width = 128 if self.tall else size // 2
        self.block = (352 if self.tall else 64, self.width)

    def columns(self, c, x):
        start = c * 512 + x * 256 + self.start if self.tall else self.start + c * self.width
        return pl.ds(pl.multiple_of(start, 128), self.width)

    def quarter(self, sums, c, x):
        if self.tall:
            return sums.at[c, x, self.start // 128]
        return sums.at[x, :, self.columns(c, x)]

    def half(self, sums, c):
        if self.tall:
            return sums.at[c, :, self.start // 128]
        return sums.at[:, :, self.columns(c, 0)]


def share_items():
    order = [(GATE, 2048, 768, True), (DOWN, 0, 128, False), (DOWN, 128, 128, True)]
    order += [(GATE, 0, 1024, False), (GATE, 1024, 1024, True)]
    order += [(UP, 0, 1024, True), (UP, 1024, 1024, False), (UP, 2048, 768, False)]
    order += [(OUT, 0, 1024, True), (QUERY, 0, 1024, False), (KEY, 0, 1024, True)]
    order += [(VALUE, 0, 768, True), (VALUE, 768, 256, False)]
    return [Share(*item) for item in order]


def plus(left, right):
    return left + right


def dot_tn(left, right):
    return lax.dot_general(
        left, right, (((0,), (0,)), ((), ())), preferred_element_type=jnp.float32
    )


BACKWARD_IN = (
    "query",
    "key",
    "value",
    "lse",
    "h_t",
    "h2_t",
    "att_t",
    "d_b",
    "d_res",
    "d_proj",
    "g_ffn",
    "gain",
)


class Backward:
    def __init__(self, refs):
        self.__dict__.update(refs)

    def prepare(self):
        length = self.length[0, 0]
        for block in range(4):
            rows = slice(128 * block, 128 * block + 128)
            place_k = lax.broadcasted_iota(jnp.int32, (128, 512), 0) + 128 * block
            place_q = lax.broadcasted_iota(jnp.int32, (128, 512), 1)
            same = (place_q >= length) == (place_k >= length)
            allowed = same & (place_k <= place_q)
            self.bias[rows, :] = jnp.where(allowed, 0.0, NEGATIVE)

    def multiply(self, left_t, right, item, target, core):
        columns = item.columns(core, 0)

        def rows(m, _):
            product = dot(left_t[tile(m, 256), :], right[:, columns]).astype(jnp.bfloat16)
            product = product.reshape(2, 2, 64, item.width)
            for xx in (0, 1):
                target[xx, m] = product[:, xx]
            return 0

        lax.fori_loop(0, 4, rows, 0)

    def multiply_tall(self, left, right, groups):
        def rows(m, _):
            at = tile(m, 256)
            turned = left[:, at].T
            for columns, targets in groups:
                product = dot(turned, right[:, columns]).astype(jnp.bfloat16)
                for n, (target, xx) in enumerate(targets):
                    target.reshape(2, 2816, 128)[xx, at, :] = product[:, 128 * n : 128 * n + 128]
            return 0

        lax.fori_loop(0, 11, rows, 0)

    def attend_back(self, first, last):
        low = jnp.bfloat16

        def pair(p, _):
            at = tile(p, 128)
            wo_rows = self.w_rows[p].reshape(128, 1024)
            grad = dot_nt(self.d_proj[...], wo_rows).astype(low)
            query = (self.query[:, at].astype(jnp.float32) * SCORE_SCALE).astype(low)
            key, value = self.key[:, at], self.value[:, at]
            left = lax.broadcasted_iota(jnp.int32, (512, 128), 1) < HEAD
            none = jnp.zeros((512, 128), low)
            sides = [
                [jnp.where(side, v, none) for v in (query, key, value, grad)]
                for side in (left, ~left)
            ]
            grad_key, grad_value = [None, None], [None, None]
            for block in (0, 1):
                rows, seen = slice(256 * block, 256 * block + 256), slice(0, 256 * block + 256)
                grad_query = None
                parts_key, parts_value = None, None
                for n, (own_query, own_key, own_value, own_grad) in enumerate(sides):
                    self.d_in[seen, 0:256] = dot_nt(own_key[seen], query[rows])
                    self.d_in[seen, 256:512] = dot_nt(own_value[seen], grad[rows])
                    self.back_rows(p, n, rows, 256 * block + 256)
                    grad_scores, probs = self.grad_scores[seen, :], self.probs[seen, :]
                    part_query = dot_tn(grad_scores, own_key[seen])
                    part_key = dot(grad_scores, own_query[rows])
                    part_value = dot(probs, own_grad[rows])
                    if n == 0:
                        grad_query, parts_key, parts_value = part_query, part_key, part_value
                    else:
                        grad_query += part_query
                        parts_key += part_key
                        parts_value += part_value
                self.query[rows, at] = (grad_query * SCORE_SCALE).astype(low)
                if block == 0:
                    grad_key[0], grad_value[0] = parts_key, parts_value
                else:
                    grad_key = [grad_key[0] + parts_key[:256], parts_key[256:]]
                    grad_value = [grad_value[0] + parts_value[:256], parts_value[256:]]
            for block in (0, 1):
                rows = slice(256 * block, 256 * block + 256)
                self.key[rows, at] = grad_key[block].astype(low)
                self.value[rows, at] = grad_value[block].astype(low)
            return 0

        lax.fori_loop(first, last, pair, 0)

    def back_rows(self, p, n, rows, count):
        low = jnp.bfloat16
        held = self.d_in
        lse = self.lse[p, n : n + 1, rows]

        def first_pass(r, centre):
            keys = tile(r, 64)
            probs = jnp.exp(held[keys, 0:256] + self.bias[keys, rows] - lse)
            held[keys, 0:256] = probs
            self.probs[keys, :] = probs.astype(low)
            return centre + jnp.sum((held[keys, 256:512] * probs).reshape(8, 8, 256), axis=0)

        centre = lax.fori_loop(0, count // 64, first_pass, jnp.zeros((8, 256), jnp.float32), unroll=2)
        centre = jnp.sum(centre, axis=0, keepdims=True)

        def second_pass(r, _):
            keys = tile(r, 64)
            grad = held[keys, 0:256] * (held[keys, 256:512] - centre)
            self.grad_scores[keys, :] = grad.astype(low)
            return 0

        lax.fori_loop(0, count // 64, second_pass, 0, unroll=2)

    def grad_hidden(self, t):
        at = pl.ds(256 * t, 256)
        total = None
        for n, grad in enumerate((self.query, self.key, self.value)):
            part = dot_nt(grad[...], self.w_rows[2 * n : 2 * n + 2].reshape(256, 1024))
            total = part if total is None else total + part
        self.d_in[:, at] = total

    def finish(self):
        self.gain_total[...] = jnp.zeros_like(self.gain_total)

        def rows_of(block, _):
            rows = tile(block, 64)
            values = self.tokens[rows, :].astype(jnp.float32)
            factor = lax.rsqrt(jnp.mean(values * values, axis=-1, keepdims=True) + NORM_EPS)
            normed = values * factor
            grad = self.d_in[rows, :]
            self.gain_total[...] += jnp.sum((grad * normed).reshape(8, 8, 1024), axis=0)
            grad_normed = grad * self.gain[0:1, :].astype(jnp.float32)
            mean = jnp.mean(grad_normed * normed, axis=-1, keepdims=True)
            self.d_in[rows, :] = self.d_res[rows, :] + factor * (
                grad_normed - normed * mean
            )
            return 0

        lax.fori_loop(0, 8, rows_of, 0)
        self.gain_lines[...] = jnp.zeros_like(self.gain_lines)
        lines = [jnp.sum(v[...], axis=0, keepdims=True) for v in (self.gain_total, self.g_ffn)]
        for s in range(8):
            for n, line in enumerate(lines):
                self.gain_lines[s // 2, s % 2, n : n + 1] = line[:, 128 * s : 128 * s + 128]


def backward_kernel(items, *refs):
    refs = list(refs)

    def take(n):
        taken = refs[:n]
        del refs[:n]
        return taken

    kept = take(len(KEPT))
    middle_in, grad_gate_in, grad_up_in = take(3)
    saved_in = dict(zip(BACKWARD_IN, take(len(BACKWARD_IN))))
    tokens_in, length = take(2)
    sums = take(7)
    gain_sums, input_grad_out = take(2)
    saved = dict(zip(BACKWARD_IN, take(len(BACKWARD_IN))))
    d_in, wide, w_rows, bias, probs, grad_scores, gain_total, gain_lines = take(8)
    mine, from_first, from_second, from_z = (take(len(items)) for _ in range(4))
    ring, tall_ring = take(RING), take(2)
    outbox, tall_outbox = take(2), take(2)
    gain_core, gain_x, gain_y, gain_z = take(4)
    send_sems, recv_sems, load_sems, credit = refs
    z, y, x, c = place()
    far = [lax.rem(z + k, 4) for k in range(4)]
    back = [lax.rem(z + 4 - k, 4) for k in range(4)]
    x_other, y_other, c_other = (
        device(z, y, 1 - x, c),
        device(z, 1 - y, x, c),
        device(z, y, x, 1 - c),
    )
    loads = {}

    def load(name, source, target):
        loads[name] = pltpu.make_async_copy(source, target, load_sems.at[len(loads)])
        loads[name].start()

    waited = set()

    def loaded(*names):
        for name in names:
            if name not in waited:
                loads[name].wait()
                waited.add(name)

    load("d_gate", grad_gate_in, wide.at[1])
    load("h2_t", saved_in["h2_t"], saved["h2_t"])
    load("mid", middle_in, wide.at[0])
    load("d_b", saved_in["d_b"], saved["d_b"])
    load("wo_rows", kept[OUT].reshape(8, 2, 64, 1024), w_rows)
    for name in BACKWARD_IN:
        if name not in loads:
            load(name, saved_in[name], saved[name])
    greet()
    wires = Wires(send_sems, recv_sems)
    work = Backward(
        dict(
            saved,
            tokens=saved["d_b"],
            length=length,
            w_rows=w_rows,
            probs=probs,
            grad_scores=grad_scores,
            bias=bias,
            d_in=d_in,
            gain_total=gain_total,
            gain_lines=gain_lines,
        )
    )
    tall_items = [i for i, item in enumerate(items) if item.tall]
    wide_items = [i for i, item in enumerate(items) if not item.tall]

    def slot(i, k):
        return SUM_SLOTS * i + k

    def core_slots(i):
        return (slot(i, 0), slot(i, 8))

    def from_core(i):
        if items[i].tall:
            return tall_ring[tall_items.index(i)]
        return ring[wide_items.index(i) % RING].at[..., : items[i].width]

    def produce(i):
        item = items[i]
        if item.tall:
            number = tall_items.index(i)
            if number == 0:
                loaded("mid", "d_b")
                groups = []
                for core, boxes in ((1 - c, tall_outbox), (c, [mine[j] for j in tall_items])):
                    columns = pl.ds(pl.multiple_of(512 * core, 512), 512)
                    groups.append((columns, [(boxes[j], xx) for xx in (0, 1) for j in (0, 1)]))
                work.multiply_tall(wide.at[0], saved["d_b"], groups)
                load("d_up", grad_up_in, wide.at[0])
                load("tokens", tokens_in, saved["d_b"])
            box = tall_outbox[number]
        else:
            number = wide_items.index(i)
            if number >= 2:
                wires.finish(lambda s: s in core_slots(wide_items[number - 2]))
            box = outbox[number % 2].at[..., : item.width]
            left, right, names = {
                GATE: (saved["h2_t"], wide.at[1], ("h2_t", "d_gate")),
                UP: (saved["h2_t"], wide.at[0], ("d_up",)),
                OUT: (saved["att_t"], saved["d_proj"], ("att_t", "d_proj")),
                QUERY: (saved["h_t"], saved["query"], ("h_t",)),
                KEY: (saved["h_t"], saved["key"], ()),
                VALUE: (saved["h_t"], saved["value"], ()),
            }[item.weight]
            loaded(*names)
            multiply = partial(work.multiply, left, right, item)
            if number >= RING:
                pl.semaphore_wait(credit, 1)
            multiply(box, 1 - c)
        for xx in (0, 1):
            wires.send(core_slots(i)[xx], box.at[xx], from_core(i).at[xx], c_other)
        if not item.tall:
            multiply(mine[i], c)

    def first_hop(i):
        item, own, other = items[i], mine[i], from_core(i)
        for xx in (0, 1):
            wires.arrived(core_slots(i)[xx], other.at[xx])

        def add(at, _):
            for xx in (0, 1):
                for yy in (0, 1):
                    own[xx, at, yy] = plus(own[xx, at, yy], other[xx, at, yy])
            return 0

        lax.fori_loop(0, 4, add, 0)
        if not item.tall and wide_items.index(i) + RING < len(wide_items):
            pl.semaphore_signal(credit, inc=1, device_id=c_other, device_id_type=MESH)
        if item.x_first:
            wires.send(slot(i, 1), own.at[1 - x], from_first[i], x_other)
        else:
            wires.send(slot(i, 1), own.at[:, :, 1 - y], from_first[i], y_other)

    def second_hop(i):
        item, own, other = items[i], mine[i], from_first[i]
        wires.arrived(slot(i, 1), other)

        def add(at, _):
            for side in (0, 1):
                if item.x_first:
                    own[x, at, side] = plus(own[x, at, side], other[at, side])
                else:
                    own[side, at, y] = plus(own[side, at, y], other[side, at])
            return 0

        lax.fori_loop(0, 4, add, 0)
        if item.x_first:
            wires.send(slot(i, 2), own.at[x, :, 1 - y], from_second[i], y_other)
        else:
            to_z(i, lambda k: own.at[:, far[k], y])

    def to_z(i, block):
        for k in (1, 2, 3):
            wires.send(slot(i, 2 + k), block(k), from_z[i].at[k - 1], device(far[k], y, x, c))

    def z_total(i, own_part):
        total = own_part.astype(jnp.float32)
        for k in (1, 2, 3):
            wires.arrived(slot(i, 2 + k), from_z[i].at[k - 1])
            total += from_z[i][k - 1].astype(jnp.float32)
        return total.astype(jnp.bfloat16)

    def third_hop(i):
        item, own, other = items[i], mine[i], from_second[i]
        if not item.x_first:
            own[:, z, y] = z_total(i, own[:, z, y])
            wires.send(slot(i, 2), own.at[:, z, y], other, x_other)
            return
        wires.arrived(slot(i, 2), other)

        def add(at, _):
            own[x, at, y] = plus(own[x, at, y], other[at])
            return 0

        lax.fori_loop(0, 4, add, 0)
        to_z(i, lambda k: own.at[x, far[k], y])

    def fourth_hop(i):
        item, own = items[i], mine[i]
        if not item.x_first:
            wires.arrived(slot(i, 2), from_second[i])
            block = item.half(sums[item.weight], c)
            block[...] = plus(own[:, z, y], from_second[i][...])
            wires.send(slot(i, 7), block, block, c_other)
            return
        block = item.quarter(sums[item.weight], c, x)
        block[...] = z_total(i, own[x, z, y])
        wires.send(slot(i, 6), block, block, x_other)

    def to_sibling(i):
        item = items[i]
        if item.x_first:
            wires.arrived(slot(i, 6), item.quarter(sums[item.weight], c, 1 - x))
            block = item.half(sums[item.weight], c)
            wires.send(slot(i, 7), block, block, c_other)

    def complete(i):
        item = items[i]
        wires.arrived(slot(i, 7), item.half(sums[item.weight], 1 - c))
        wires.finish(lambda s: s // SUM_SLOTS == i)

    base = SUM_SLOTS * len(items)

    def gains_one():
        wires.send(base, gain_lines, gain_core, c_other)

    def gains_two():
        wires.arrived(base, gain_core)
        gain_core[...] = gain_lines[...] + gain_core[...]
        wires.send(base + 1, gain_core, gain_x, x_other)

    def gains_three():
        wires.arrived(base + 1, gain_x)
        gain_x[...] = gain_core[...] + gain_x[...]
        wires.send(base + 2, gain_x.at[:, 1 - y], gain_y, y_other)

    def gains_four():
        wires.arrived(base + 2, gain_y)
        gain_y[...] = gain_x[:, y] + gain_y[...]
        for k in (1, 2, 3):
            wires.send(base + 2 + k, gain_y.at[far[k]], gain_z.at[z], device(far[k], y, x, c))
        gain_z[z] = gain_y[z]

    def gains_five():
        for k in (1, 2, 3):
            wires.arrived(base + 2 + k, gain_z.at[back[k]])
        gain_sums[...] = (gain_z[0] + gain_z[1]) + (gain_z[2] + gain_z[3])

    def fetch_rows(t):
        for n in range(3):
            load(("rows", n, t), kept[n].at[t], w_rows.at[2 * n : 2 * n + 2])

    def attend_back(p):
        if p == 0:
            loaded("query", "key", "value", "lse", "d_proj", "wo_rows")
        work.attend_back(p, p + 1)
        if p == 7:
            fetch_rows(0)

    def grad_hidden(t):
        loaded(*[("rows", n, t) for n in range(3)])
        work.grad_hidden(t)
        if t < 3:
            fetch_rows(t + 1)

    def finish():
        loaded("tokens", "d_res", "g_ffn", "gain")
        work.finish()
        load("d_in", d_in, input_grad_out)
        gains_one()

    beside = {1: [work.prepare]}
    for p in range(8):
        beside.setdefault(1 + p, []).append(partial(attend_back, p))
    for t in range(4):
        beside.setdefault(9 + t // 2, []).append(partial(grad_hidden, t))
    beside.setdefault(11, []).append(finish)
    for n, task in enumerate((gains_two, gains_three, gains_four, gains_five)):
        beside.setdefault(13 + 2 * n, []).append(task)

    stages = (complete, to_sibling, fourth_hop, third_hop, second_hop, first_hop, produce)
    lates = (12, 10, 8, 6, 4, 2, 0)
    for step in range(len(items) + lates[0]):
        for late, stage in zip(lates, stages):
            if 0 <= step - late < len(items):
                stage(step - late)
        for task in beside.get(step, []):
            task()
    loaded("d_in")
    wires.finish()


def backward(tokens, lengths, kept, saved):
    items = share_items()
    low, wide = jnp.bfloat16, jnp.float32
    dtypes = {name: (shape, dtype) for name, shape, dtype in FORWARD_OUTS}
    shapes = [
        jax.ShapeDtypeStruct((2, 2, 2, 352, 128) if n is None else (2, 64, n), low) for n in COLUMNS
    ]
    shapes += [jax.ShapeDtypeStruct((8, 128), wide), jax.ShapeDtypeStruct((512, 1024), wide)]
    count = SUM_SLOTS * len(items) + 6
    anywhere = pl.BlockSpec(memory_space=pl.ANY)
    in_vmem = pl.BlockSpec(memory_space=pltpu.VMEM)
    n_loads = 6 + len(BACKWARD_IN) + 12

    def buffers(lead_of):
        return [pltpu.VMEM(lead_of(item) + item.block, low) for item in items]

    out = pl.pallas_call(
        partial(backward_kernel, items),
        out_shape=shapes,
        in_specs=[anywhere] * (len(KEPT) + 3 + len(BACKWARD_IN) + 1)
        + [pl.BlockSpec(memory_space=pltpu.SMEM)],
        out_specs=[in_vmem] * 8 + [anywhere],
        scratch_shapes=[pltpu.VMEM(*dtypes[name]) for name in BACKWARD_IN]
        + [
            pltpu.VMEM((512, 1024), wide),
            pltpu.VMEM((2, 512, 2816), low),
            pltpu.VMEM((8, 2, 64, 1024), low),
            pltpu.VMEM((512, 512), wide),
            pltpu.VMEM((512, 256), low),
            pltpu.VMEM((512, 256), low),
            pltpu.VMEM((8, 1024), wide),
            pltpu.VMEM((4, 2, 8, 128), wide),
        ]
        + buffers(lambda item: (2, 4, 2))
        + buffers(lambda item: (4, 2) if item.x_first else (2, 4))
        + buffers(lambda item: (4,) if item.x_first else (2,))
        + buffers(lambda item: (3,) if item.x_first else (3, 2))
        + [pltpu.VMEM((2, 4, 2, 64, 512), low)] * RING
        + [pltpu.VMEM((2, 4, 2, 352, 128), low)] * 2
        + [pltpu.VMEM((2, 4, 2, 64, 512), low)] * 2
        + [pltpu.VMEM((2, 4, 2, 352, 128), low)] * 2
        + [
            pltpu.VMEM((4, 2, 8, 128), wide),
            pltpu.VMEM((4, 2, 8, 128), wide),
            pltpu.VMEM((4, 8, 128), wide),
            pltpu.VMEM((4, 8, 128), wide),
            pltpu.SemaphoreType.DMA((count,)),
            pltpu.SemaphoreType.DMA((count,)),
            pltpu.SemaphoreType.DMA((n_loads,)),
            pltpu.SemaphoreType.REGULAR,
        ],
        compiler_params=pltpu.CompilerParams(
            collective_id=1, has_side_effects=True, vmem_limit_bytes=63 * MIB
        ),
        name="backward_sum",
    )(
        *kept,
        saved["mid"],
        saved["d_gate"],
        saved["d_up"],
        *[saved[name] for name in BACKWARD_IN],
        tokens,
        lengths,
    )
    return out[:7], out[7], out[8]


def unpack_kernel(*refs):
    blocks, (gain_sums, mixed, d_in) = refs[:7], refs[7:10]
    sums, (gain_attn, gain_ffn, mixed_out, input_out) = refs[10:17], refs[17:21]
    held, wide = refs[21:28], refs[28:35]
    mixed_held, input_held, in_sems, out_sems = refs[35:]
    sources = (d_in, mixed, *blocks)
    places = (input_held, mixed_held, *held)
    results = (input_held, mixed_held, *wide)
    targets = (input_out, mixed_out, *sums)
    ins = [pltpu.make_async_copy(a, b, in_sems.at[n]) for n, (a, b) in enumerate(zip(sources, places))]
    outs = [pltpu.make_async_copy(a, b, out_sems.at[n]) for n, (a, b) in enumerate(zip(results, targets))]
    order = (6, 7, 8, 2, 3, 4, 5, 0, 1)
    for n in order:
        ins[n].start()
    for n in order:
        ins[n].wait()
        if n == 8:
            for b in range(8):
                wide[6][:, 128 * b : 128 * b + 128] = held[6][b // 4, b // 2 % 2, b % 2].astype(
                    jnp.float32
                )
        elif n >= 2:
            wide[n - 2][...] = held[n - 2][...].astype(jnp.float32)
        outs[n].start()
    gain_attn[...] = gain_sums[0:1]
    gain_ffn[...] = gain_sums[1:2]
    for n in order:
        outs[n].wait()


def unpack(blocks, gain_sums, mixed, d_in):
    wide = jnp.float32
    anywhere = pl.BlockSpec(memory_space=pl.ANY)
    in_vmem = pl.BlockSpec(memory_space=pltpu.VMEM)
    shapes = [
        jax.ShapeDtypeStruct((352, 1024) if n is None else (2, 64, n), wide) for n in COLUMNS
    ]
    held = [pltpu.VMEM(b.shape, b.dtype) for b in blocks]
    held += [pltpu.VMEM(v.shape, wide) for v in shapes]
    held += [pltpu.VMEM(v.shape, v.dtype) for v in (mixed, d_in)]
    shapes += [jax.ShapeDtypeStruct((1, 128), wide)] * 2
    shapes += [jax.ShapeDtypeStruct(v.shape, v.dtype) for v in (mixed, d_in)]
    out = pl.pallas_call(
        unpack_kernel,
        out_shape=shapes,
        in_specs=[anywhere] * 7 + [in_vmem] + [anywhere] * 2,
        out_specs=[anywhere] * 7 + [in_vmem] * 2 + [anywhere] * 2,
        scratch_shapes=held + [pltpu.SemaphoreType.DMA((9,)), pltpu.SemaphoreType.DMA((9,))],
        compiler_params=pltpu.CompilerParams(vmem_limit_bytes=62 * MIB),
        name="unpack",
    )(*blocks, gain_sums, mixed, d_in)
    sums = [s.reshape(-1, s.shape[-1]) for s in out[:7]]
    return sums, [g.reshape(128) for g in out[7:9]], out[9], out[10]


def gather_plain(weights, gains):
    everything = (*weights, *gains)
    whole = [lax.all_gather(v, "dp", axis=0, tiled=True) for v in everything]
    return whole[: len(weights)], whole[len(weights) :]


def sum_plain(grads, gain_grads):
    shares = [
        lax.psum_scatter(g.astype(jnp.float32), "dp", scatter_dimension=0, tiled=True)
        for g in (*grads, *gain_grads)
    ]
    sums = [lax.psum(s, ("rep", "cores")) for s in shares]
    return sums[: len(grads)], sums[len(grads) :]


def on_any_device(
    tokens,
    norm_attn,
    w_query,
    w_key,
    w_value,
    w_out,
    norm_ffn,
    w_gate,
    w_up,
    w_down,
    lengths,
    cotangent,
):
    rows = tokens.shape[0]
    low = jnp.bfloat16
    allowed, valid = masks(lengths, rows)
    whole, gains = gather_plain(
        (w_query, w_key, w_value, w_out, w_gate, w_up, w_down), (norm_attn, norm_ffn)
    )
    full_query, full_key, full_value, full_out, full_gate, full_up, full_down = whole
    gain_attn, gain_ffn = gains
    inputs = tokens.astype(jnp.float32)
    normed, factor = normalize(inputs)
    hidden = (normed * gain_attn.astype(jnp.float32)).astype(low)
    query = matmul(hidden, full_query).astype(low)
    keyed = matmul(hidden, full_key).astype(low)
    valued = matmul(hidden, full_value).astype(low)
    query_groups, key_groups, value_groups = (to_groups(query), to_groups(keyed), to_groups(valued))
    attended_groups, log_total = lax.map(
        partial(attend, allowed), (query_groups, key_groups, value_groups)
    )
    attended = from_groups(attended_groups)
    residual = inputs + matmul(attended, full_out)
    normed_two, factor_two = normalize(residual)
    hidden_two = (normed_two * gain_ffn.astype(jnp.float32)).astype(low)
    gate = matmul(hidden_two, full_gate)
    upward = matmul(hidden_two, full_up)
    sigma = jax.nn.sigmoid(gate)
    middle = (gate * sigma * upward).astype(low)
    mixed = (valid[:, None] * (residual + matmul(middle, full_down))).astype(low)
    grad_output = cotangent.astype(jnp.float32) * valid[:, None]
    grad_branch = grad_output.astype(low)
    grad_down = matmul_tn(middle, grad_branch)
    grad_middle = matmul_nt(grad_branch, full_down)
    grad_gate_rows = (grad_middle * upward * sigma * (1.0 + gate * (1.0 - sigma))).astype(low)
    grad_up_rows = (grad_middle * gate * sigma).astype(low)
    grad_gate = matmul_tn(hidden_two, grad_gate_rows)
    grad_up = matmul_tn(hidden_two, grad_up_rows)
    grad_hidden_two = matmul_nt(grad_gate_rows, full_gate) + matmul_nt(grad_up_rows, full_up)
    grad_gain_ffn = jnp.sum(grad_hidden_two * normed_two, axis=0)
    grad_residual = grad_output + norm_back(
        grad_hidden_two * gain_ffn.astype(jnp.float32), normed_two, factor_two
    )
    grad_proj = grad_residual.astype(low)
    grad_out = matmul_tn(attended, grad_proj)
    grad_attended = matmul_nt(grad_proj, full_out).astype(low)
    grad_query_g, grad_key_g, grad_value_g = lax.map(
        partial(attend_back, allowed),
        (query_groups, key_groups, value_groups, to_groups(grad_attended), log_total),
    )
    grad_query_rows = from_groups(grad_query_g)
    grad_key_rows = from_groups(grad_key_g)
    grad_value_rows = from_groups(grad_value_g)
    grad_query = matmul_tn(hidden, grad_query_rows)
    grad_key = matmul_tn(hidden, grad_key_rows)
    grad_value = matmul_tn(hidden, grad_value_rows)
    grad_hidden = (
        matmul_nt(grad_query_rows, full_query)
        + matmul_nt(grad_key_rows, full_key)
        + matmul_nt(grad_value_rows, full_value)
    )
    grad_gain_attn = jnp.sum(grad_hidden * normed, axis=0)
    input_grad = grad_residual + norm_back(
        grad_hidden * gain_attn.astype(jnp.float32), normed, factor
    )
    grads = (grad_query, grad_key, grad_value, grad_out, grad_gate, grad_up, grad_down)
    sums, gain_sums = sum_plain([g.astype(low) for g in grads], (grad_gain_attn, grad_gain_ffn))
    return (
        mixed,
        input_grad,
        gain_sums[0],
        sums[0],
        sums[1],
        sums[2],
        sums[3],
        gain_sums[1],
        sums[4],
        sums[5],
        sums[6],
    )


def on_tuned_device(
    tokens,
    norm_attn,
    w_query,
    w_key,
    w_value,
    w_out,
    norm_ffn,
    w_gate,
    w_up,
    w_down,
    lengths,
    cotangent,
):
    weights = (w_query, w_key, w_value, w_out, w_gate, w_up, w_down)
    kept, saved = forward(tokens, cotangent, lengths, weights, (norm_attn, norm_ffn))
    blocks, gain_lines, d_in = backward(tokens, lengths, kept, saved)
    sums, gain_sums, mixed, d_in = unpack(blocks, gain_lines, saved["mixed"], d_in)
    return (
        mixed,
        d_in,
        gain_sums[0],
        *sums[:4],
        gain_sums[1],
        *sums[4:],
    )


def solution(mesh):
    tuned = dict(mesh.shape) == {"dp": 8, "rep": 2, "cores": 2}
    tokens_placed = P(("dp", "rep", "cores"), None)
    share, gain = P("dp", None), P("dp")
    return jax.shard_map(
        on_tuned_device if tuned else on_any_device,
        mesh=mesh,
        in_specs=(
            tokens_placed,
            gain,
            share,
            share,
            share,
            share,
            gain,
            share,
            share,
            share,
            tokens_placed,
            tokens_placed,
        ),
        out_specs=(
            tokens_placed,
            tokens_placed,
            gain,
            share,
            share,
            share,
            share,
            gain,
            share,
            share,
            share,
        ),
        check_vma=False,
    )
```

profile of v0, /device:TPU:0, one launch (start us, length us, event | category | flops | bytes accessed | tf_op | source)
XLA Modules:
  0.0 300.6 jit_solution(8882474888221900357)
XLA Ops:
  1.3 135.7 %gather_forward.1 = (bf16[4,2,2,64,1024]{4,3,2,1,0:T(8,128)(2,1)}, bf16[4,2,2,64,1024]{4,3,2,1,0:T(8,128)(2,1)}, bf16[4,2,2,64,1024]{4,3,2,1,0:T(8,128)(2,1)}, b...) custom-call(bf16[2,64,1024]{2,1,0:T(8,128)(2,1)} %bitcast.18, ...), custom_call_target="tpu_custom_call" | custom-call | tf_op jit(solution)/shard_map/gather_forward/pallas_call | solution.py:623
  137.0 156.6 %backward_sum.1 = (bf16[2,64,1024]{2,1,0:T(8,128)(2,1)}, bf16[2,64,1024]{2,1,0:T(8,128)(2,1)}, bf16[2,64,1024]{2,1,0:T(8,128)(2,1)}, bf16[2,64,1024]{2,1,0:T(8,1...) custom-call(bf16[4,2,2,64,1024]{4,3,2,1,0:T(8,128)(2,1)} %get-tuple-, ...), custom_call_target="tpu_custom_call" | custom-call | tf_op jit(solution)/shard_map/backward_sum/pallas_call | solution.py:1143
  293.6 6.8 %unpack.1 = (f32[2,64,1024]{2,1,0:T(8,128)}, f32[2,64,1024]{2,1,0:T(8,128)}, f32[2,64,1024]{2,1,0:T(8,128)}, f32[2,64,1024]{2,1,0:T(8,128)}, f32[2,64,2816]{2,1,...) custom-call(bf16[2,64,1024]{2,1,0:T(8,128)(2,1)} %get-tuple-element., ...), custom_call_target="tpu_custom_call" | custom-call | tf_op jit(solution)/shard_map/unpack/pallas_call | solution.py:1236
where the time goes:
time: 306 us; the launch traced here: 301 us
  Pallas kernels  299 us (98%)
    pallas_call x1, Pallas kernels, backward(): pl.pallas_call(partial(backward_kernel, items), out_shape=shapes, in_spec...  157 us
    pallas_call x1, Pallas kernels, forward(): pl.pallas_call(partial(forward_kernel, items), out_shape=shapes, in_specs...  136 us
    pallas_call x1, Pallas kernels, unpack(): pl.pallas_call(unpack_kernel, out_shape=shapes, in_specs=[anywhere] * 7 +...  6.8 us

commit v1 on v0

--- a/solution.py
+++ b/solution.py
@@ -183,7 +183,7 @@
 
 
 GATHER_SLOTS = 12
-LAG = 2
+LAG = 3
 ALL = slice(None)
 COLUMNS = (1024, 1024, 1024, 1024, 2816, 2816, None)
 QUERY, KEY, VALUE, OUT, GATE, UP, DOWN = range(7)
@@ -585,8 +585,8 @@
         wires.arrived(gain_slot + k, full_gains.at[back[k], y])
     wires.send(gain_slot, full_gains.at[:, y], full_gains.at[:, y], y_other)
     stages = (retire, complete, last_hop, second_hop, first_hop)
-    lates = (3 * LAG, 3 * LAG - 1, 2 * LAG, LAG, 0)
-    for step in range(len(items) + 3 * LAG):
+    lates = (2 * LAG + 2, 2 * LAG + 1, 2 * LAG, LAG, 0)
+    for step in range(len(items) + lates[0]):
         for late, stage in zip(lates, stages):
             if 0 <= step - late < len(items):
                 stage(step - late)
@@ -1113,7 +1113,7 @@
         beside.setdefault(13 + 2 * n, []).append(task)
 
     stages = (complete, to_sibling, fourth_hop, third_hop, second_hop, first_hop, produce)
-    lates = (12, 10, 8, 6, 4, 2, 0)
+    lates = (16, 14, 12, 9, 6, 3, 0)
     for step in range(len(items) + lates[0]):
         for late, stage in zip(lates, stages):
             if 0 <= step - late < len(items):

time: 306 us -> 307 us (level)
  no operation moved by 1% of the time
where the time goes in v1:
time: 307 us; the launch traced here: 302 us
  Pallas kernels  300 us (98%)
    pallas_call x1, Pallas kernels, backward(): pl.pallas_call(partial(backward_kernel, items), out_shape=shapes, in_spec...  158 us
    pallas_call x1, Pallas kernels, forward(): pl.pallas_call(partial(forward_kernel, items), out_shape=shapes, in_specs...  135 us
    pallas_call x1, Pallas kernels, unpack(): pl.pallas_call(unpack_kernel, out_shape=shapes, in_specs=[anywhere] * 7 +...  6.8 us

profile of v1, /device:TPU:0, one launch (start us, length us, event | category | flops | bytes accessed | tf_op | source)
XLA Modules:
  0.0 301.7 jit_solution(8295441357377306706)
XLA Ops:
  1.3 135.3 %gather_forward.1 = (bf16[4,2,2,64,1024]{4,3,2,1,0:T(8,128)(2,1)}, bf16[4,2,2,64,1024]{4,3,2,1,0:T(8,128)(2,1)}, bf16[4,2,2,64,1024]{4,3,2,1,0:T(8,128)(2,1)}, b...) custom-call(bf16[2,64,1024]{2,1,0:T(8,128)(2,1)} %bitcast.18, ...), custom_call_target="tpu_custom_call" | custom-call | tf_op jit(solution)/shard_map/gather_forward/pallas_call | solution.py:623
  136.6 158.0 %backward_sum.1 = (bf16[2,64,1024]{2,1,0:T(8,128)(2,1)}, bf16[2,64,1024]{2,1,0:T(8,128)(2,1)}, bf16[2,64,1024]{2,1,0:T(8,128)(2,1)}, bf16[2,64,1024]{2,1,0:T(8,1...) custom-call(bf16[4,2,2,64,1024]{4,3,2,1,0:T(8,128)(2,1)} %get-tuple-, ...), custom_call_target="tpu_custom_call" | custom-call | tf_op jit(solution)/shard_map/backward_sum/pallas_call | solution.py:1143
  294.7 6.8 %unpack.1 = (f32[2,64,1024]{2,1,0:T(8,128)}, f32[2,64,1024]{2,1,0:T(8,128)}, f32[2,64,1024]{2,1,0:T(8,128)}, f32[2,64,1024]{2,1,0:T(8,128)}, f32[2,64,2816]{2,1,...) custom-call(bf16[2,64,1024]{2,1,0:T(8,128)(2,1)} %get-tuple-element., ...), custom_call_target="tpu_custom_call" | custom-call | tf_op jit(solution)/shard_map/unpack/pallas_call | solution.py:1236
